TPU v7x, 32 devices: a whole 2x2x4 slice. The times are simulated.
32 devices in a mesh: parts: 2 (over y), tm: 4 (over z), factor: 4 (over x, core).
Axes of the slice: x: 2, y: 2, z: 4, core: 2. Of those that a mesh axis runs over, the one named last changes fastest.
Arguments:
- schur_matrix: float32 [24576, 24, 4, 128], P(('parts', 'tm'), None, 'factor'), parts along dimension 0, as said below
- link_rhs: float32 [24576], P(('parts', 'tm')), parts along dimension 0, may hold values from -6 to 6
- hour_rhs: float32 [32, 256], P(('parts', 'tm', 'factor')), parts along dimension 0, may hold values from -6 to 6
- link_cols: int32 [32, 256], P(('parts', 'tm', 'factor')), parts along dimension 0, may hold values from 0 to 255
- link_coef: float32 [32, 256], P(('parts', 'tm', 'factor')), parts along dimension 0, may hold values from -6 to 6
- hour_inverse: float32 [32, 256, 256], P(('parts', 'tm', 'factor')), parts along dimension 0, may hold values from -0.375 to 0.375
- couple_prev: float32 [32, 2, 256], P(('parts', 'tm', 'factor')), parts along dimension 0, may hold values from -1.2 to 1.2
- couple_next: float32 [32, 2, 256], P(('parts', 'tm', 'factor')), parts along dimension 0, may hold values from -1.2 to 1.2
Outputs:
- schur_trail: float32 [24576, 24, 4, 128], P(('parts', 'tm'), None, 'factor'), parts along dimension 0
- link_trail: float32 [24576], P(('parts', 'tm')), parts along dimension 0
- hour_step: float32 [32, 256], P(('parts', 'tm', 'factor')), parts along dimension 0
There are 2 independent parts, one for each index of `parts`. A program takes and returns all parts, laid end to end along the dimension named above; each array names one. Nothing has to cross between parts.
Inputs may be any that keep to these rules, and one draw needn't show every extreme that they name: schur_matrix is symmetric and its leading 2 * 128 rows and columns form a positive definite block.
All inputs are finite; a program needn't handle non-finite values.
Results may differ from a plain program's by a relative error of at most 0.0001.
Values sent between devices are 32-bit elements; how exact they have to be, the bound alone decides.
A program may use at most 192 MiB of HBM per device.

v0:
```python
import jax
import jax.numpy as jnp
from jax import lax
from jax.sharding import PartitionSpec as P

PANELS = 2
BW = 2
SWEEPS = 2


def spread(array, axis, root):
    mine = lax.axis_index(axis) == root
    return lax.psum(jnp.where(mine, array, jnp.zeros_like(array)), axis)


def with_halo(cells, sides, width):
    for axis, dim in sides:
        count = lax.axis_size(axis)
        ends = count - 1
        head = lax.slice_in_dim(cells, 0, width, axis=dim)
        tail = lax.slice_in_dim(cells, cells.shape[dim] - width, cells.shape[dim], axis=dim)
        cells = jnp.concatenate(
            [
                lax.ppermute(tail, axis, [(i, (i + 1) % count) for i in range(ends)]),
                cells,
                lax.ppermute(head, axis, [((i + 1) % count, i) for i in range(ends)]),
            ],
            axis=dim,
        )
    return cells


def shards(
    schur_matrix, link_rhs, hour_rhs, link_cols, link_coef, hour_inverse, couple_prev, couple_next
):
    rows_here = schur_matrix.shape[0]
    tiles_here = schur_matrix.shape[1]
    width = schur_matrix.shape[3]
    factors = lax.axis_size("factor")
    row_start = lax.axis_index("tm") * rows_here
    global_rows = row_start + jnp.arange(rows_here, dtype=jnp.int32)
    factor_here = lax.axis_index("factor")
    schur_now = schur_matrix
    rhs_now = link_rhs
    solved = []
    for panel_id in range(PANELS):
        column_tile = panel_id // factors
        owner_index = panel_id % factors
        own_cols = schur_now[:, column_tile, 0, :]
        panel_cols = spread(own_cols, "factor", owner_index)
        panel_first = panel_id * width
        picker = (
            global_rows[:, None] - panel_first == jnp.arange(width, dtype=jnp.int32)[None, :]
        ).astype(jnp.float32)
        block_part = jnp.dot(picker.T, panel_cols, precision=lax.Precision.HIGHEST)
        rhs_part = jnp.dot(picker.T, rhs_now, precision=lax.Precision.HIGHEST)
        diag_block, rhs_segment = lax.psum((block_part, rhs_part), "tm")
        lower_block = jnp.linalg.cholesky(diag_block)
        factor_rows = jax.scipy.linalg.solve_triangular(lower_block, panel_cols.T, lower=True).T
        factor_rows = jnp.where(
            (global_rows < panel_first)[:, None], jnp.zeros_like(factor_rows), factor_rows
        )
        all_factor = lax.all_gather(factor_rows, "tm", axis=0, tiled=True)
        grouped = all_factor.reshape(tiles_here, factors, width, width)
        my_tiles = lax.dynamic_index_in_dim(grouped, factor_here, 1, keepdims=False)
        link_step = jax.scipy.linalg.solve_triangular(lower_block, rhs_segment, lower=True)
        rhs_now = rhs_now - jnp.dot(factor_rows, link_step, precision=lax.Precision.HIGHEST)
        update = jnp.einsum("rk,tck->rtc", factor_rows, my_tiles, precision=lax.Precision.HIGHEST)
        schur_now = schur_now - update[:, :, None, :]
        solved.append(link_step)
    link_values = jnp.concatenate(solved)
    one_hot = (
        link_cols[:, :, None] == jnp.arange(PANELS * width, dtype=jnp.int32)[None, None, :]
    ).astype(jnp.float32)
    looked = jnp.einsum("hik,k->hi", one_hot, link_values, precision=lax.Precision.HIGHEST)
    target = hour_rhs - link_coef * looked
    hour_state = jnp.einsum("hik,hk->hi", hour_inverse, target, precision=lax.Precision.HIGHEST)
    for sweep_id in range(SWEEPS):
        border_pairs = jnp.concatenate((hour_state[:, :BW], hour_state[:, -BW:]), axis=1)
        padded = with_halo(border_pairs, ((("tm", "factor"), 0),), 1)
        prev_last = padded[:-2, BW:]
        next_first = padded[2:, :BW]
        coupling = jnp.einsum("hbi,hb->hi", couple_prev, prev_last, precision=lax.Precision.HIGHEST)
        coupling = coupling + jnp.einsum(
            "hbi,hb->hi", couple_next, next_first, precision=lax.Precision.HIGHEST
        )
        hour_state = jnp.einsum(
            "hik,hk->hi", hour_inverse, target - coupling, precision=lax.Precision.HIGHEST
        )
    return (schur_now, rhs_now, hour_state)


def solution(mesh):
    placed = (
        P(("parts", "tm"), None, "factor", None),
        P(("parts", "tm")),
        P(("parts", "tm", "factor"), None),
        P(("parts", "tm", "factor"), None),
        P(("parts", "tm", "factor"), None),
        P(("parts", "tm", "factor"), None, None),
        P(("parts", "tm", "factor"), None, None),
        P(("parts", "tm", "factor"), None, None),
    )
    return jax.shard_map(
        shards,
        mesh=mesh,
        in_specs=placed,
        out_specs=(
            P(("parts", "tm"), None, "factor", None),
            P(("parts", "tm")),
            P(("parts", "tm", "factor"), None),
        ),
        check_vma=False,
    )
```

profile of v0, /device:TPU:19, one launch (start us, length us, event | category | flops | bytes accessed | tf_op | source)
XLA Modules:
  0.0 658.2 jit_solution(964721345408237185)
XLA Ops:
  7.2 32.9 %copy.16 = f32[3072,24,1,128]{3,0,1,2:T(8,128)} copy(f32[3072,24,1,128]{3,2,1,0:T(1,128)} %param.13) | data formatting | bytes 75497472 | tf_op args[0]
  40.2 2.7 fusion.1
  42.9 43.3 %all-reduce.5.cloned.1.call-done = f32[3072,128]{1,0:T(8,128)} async-done(((f32[3072,128]{1,0:T(8,128)}), f32[3072,128]{1,0:T(8,128)}) %all-reduce.5.cloned.1.call-update) | async-done | bytes 1572880 | tf_op jit(solution)/shard_map/psum | solution.py:13
  86.2 4.0 fusion.8
  90.3 32.7 %all-reduce.7.cloned.1.call-done = f32[128,128]{0,1:T(8,128)} async-done(((f32[128,128]{0,1:T(8,128)}), f32[128,128]{0,1:T(8,128)}) %all-reduce.7.cloned.1.call-update) | async-done | bytes 65552 | tf_op jit(solution)/shard_map/psum | solution.py:57
  123.0 0.9 copy.13
  123.9 0.9 fusion.35
  124.8 11.7 %cholesky.44 = f32[128,128]{1,0:T(8,128)S(1)} custom-call(f32[128,128]{1,0:T(8,128)S(1)} %fusion.35), custom_call_target="Cholesky" | custom-call | tf_op jit(solution)/shard_map/jit(cholesky)/cholesky | solution.py:58
  136.5 0.6 compare_reduce_fusion.1
  137.1 0.7 fusion.26
  137.8 9.8 %custom-call.10 = f32[1,128,128]{1,2,0:T(8,128)S(1)} custom-call(f32[1,128,128]{2,1,0:T(8,128)S(1)} %fusion.26), custom_call_target="InvertDiagBlocksLowerTriangular" | custom-call | tf_op jit(solution)/shard_map/jit(_solve_triangular)/triangular_solve | solution.py:59
  147.6 2.7 convolution_select_fusion.1
  150.5 115.4 %all-gather.3.cloned.1.call-done = f32[12288,128]{0,1:T(8,128)} async-done(((f32[3072,128]{0,1:T(8,128)}), f32[12288,128]{0,1:T(8,128)}) %all-gather.3.cloned.1.call-update) | async-done | bytes 6291472 | tf_op jit(solution)/shard_map/all_gather | solution.py:63
  265.9 8.3 %reshape.109 = f32[24,4,128,128]{2,1,0,3:T(4,128)} reshape(f32[12288,128]{0,1:T(8,128)} %all-gather.3.cloned.1.call-done) | data formatting | bytes 12582912 | tf_op jit(solution)/shard_map/reshape | solution.py:64
  274.2 5.6 constant_dynamic-slice_fusion.1
  279.8 3.8 copy.14
  283.6 41.2 %bitcast_subtract_fusion.1 = f32[3072,24,1,128]{3,0,1,2:T(8,128)} fusion(f32[24,1,128,128]{3,2,0,1:T(8,128)S(1)} %copy.14, f32[128,3072]{1,0:T(8,128)S(1)} %copy-done.3, f32[3072,24,1,128]{3,2,1,0:T(1,128)} %param.13), kind=kOutput, calls=%fused_computation.1 | convolution fusion | flops 14504951808 | bytes 78643200 | tf_op jit(solution)/shard_map/rk,tck->rtc/dot_general | solution.py:68
  324.9 2.7 fusion
  327.7 42.2 %all-reduce.9.cloned.1.call-done = f32[3072,128]{1,0:T(8,128)} async-done(((f32[3072,128]{1,0:T(8,128)}), f32[3072,128]{1,0:T(8,128)}) %all-reduce.9.cloned.1.call-update) | async-done | bytes 1572880 | tf_op jit(solution)/shard_map/psum | solution.py:13
  369.9 4.0 fusion.9
  374.2 32.5 %all-reduce.11.cloned.1.call-done = f32[128,128]{0,1:T(8,128)} async-done(((f32[128,128]{0,1:T(8,128)}), f32[128,128]{0,1:T(8,128)}) %all-reduce.11.cloned.1.call-update) | async-done | bytes 65552 | tf_op jit(solution)/shard_map/psum | solution.py:57
  406.6 0.9 copy.18
  407.6 1.5 fusion.31
  409.0 12.5 %cholesky.55 = f32[128,128]{1,0:T(8,128)S(1)} custom-call(f32[128,128]{1,0:T(8,128)} %fusion.31), custom_call_target="Cholesky" | custom-call | tf_op jit(solution)/shard_map/jit(cholesky)/cholesky | solution.py:58
  421.6 0.6 compare_reduce_fusion
  422.3 1.3 fusion.27
  423.5 10.6 %custom-call.11 = f32[1,128,128]{1,2,0:T(8,128)S(1)} custom-call(f32[1,128,128]{2,1,0:T(8,128)} %fusion.27), custom_call_target="InvertDiagBlocksLowerTriangular" | custom-call | tf_op jit(solution)/shard_map/jit(_solve_triangular)/triangular_solve | solution.py:59
  434.2 2.7 convolution_select_fusion
  436.9 2.1 fusion.14
  439.1 6.1 psum.46
  445.4 0.9 fusion.55
  446.3 0.8 sub.28
  447.1 1.5 fusion.13
  448.6 9.3 %psum.47 = f32[128]{0:T(128)S(1)} all-reduce(f32[128]{0:T(128)S(1)} %fusion.13), channel_id=1, replica_groups=mesh['parts'=2,'tm'=4,'factor'=4] {'tm'}, use_global_device_ids=true, to_apply=%region_7.11 | all-reduce | flops 128 | bytes 1024 | tf_op jit(solution)/shard_map/psum | solution.py:57
  458.0 0.9 fusion.12
  459.5 8.6 %collective-permute-start.1 = (f32[1,4]{1,0:T(1,128)S(1)}, f32[1,4]{1,0:T(1,128)S(1)}, u32[]{:S(2)}, u32[]{:S(2)}) collective-permute-start(f32[1,4]{1,0:T(1,128)S(1)} %pad_maximum_fusion.1), channel_id=1, source_target_pairs={{1,0},{2,1},{3,2},{4,3},{5,4},{6,5},{7,6},{8,7},{9,8},{10,9},{11,1... | collective-permute-start | bytes 56 | tf_op jit(solution)/shard_map/ppermute | solution.py:26
  468.2 5.9 collective-permute-start
  474.1 0.9 fusion.52
  475.0 0.6 sub.29
  476.5 1.9 collective-permute-start.3
  478.4 4.8 collective-permute-start.2
  483.8 0.9 fusion.19
  484.7 68.0 %all-gather.5.cloned.1.call-done = f32[12288,128]{0,1:T(8,128)} async-done(((f32[3072,128]{0,1:T(8,128)}), f32[12288,128]{0,1:T(8,128)}) %all-gather.5.cloned.1.call-update) | async-done | bytes 6291472 | tf_op jit(solution)/shard_map/all_gather | solution.py:63
  552.7 8.3 %reshape.110 = f32[24,4,128,128]{2,1,0,3:T(4,128)} reshape(f32[12288,128]{0,1:T(8,128)} %all-gather.5.cloned.1.call-done) | data formatting | bytes 12582912 | tf_op jit(solution)/shard_map/reshape | solution.py:64
  561.0 5.6 constant_dynamic-slice_fusion
  566.6 3.7 copy.19
  570.3 37.3 %bitcast_subtract_fusion = f32[3072,24,1,128]{3,0,1,2:T(8,128)} fusion(f32[3072,24,1,128]{3,0,1,2:T(8,128)} %bitcast_subtract_fusion.1, f32[24,1,128,128]{3,2,0,1:T(8,128)S(1)} %copy.19, f32[128,3072]{1,0:T(8,128)S(1)} %copy-done.2), kind=kOutput, calls=%fused_computation | convolution fusion | flops 14504951808 | bytes 78643200 | tf_op jit(solution)/shard_map/rk,tck->rtc/dot_general | solution.py:68
  607.6 43.3 %copy.21 = f32[3072,24,1,128]{3,2,1,0:T(1,128)} copy(f32[3072,24,1,128]{3,0,1,2:T(8,128)} %bitcast_subtract_fusion) | data formatting | bytes 75497472
  (57 shorter events, 3.1 us)
Async XLA Ops:
  7.2 451.8 %copy-start = (f32[1,256,256]{2,1,0:T(8,128)S(1)}, f32[1,256,256]{2,1,0:T(8,128)}, u32[]{:S(2)}) copy-start(f32[1,256,256]{2,1,0:T(8,128)} %param.18) | copy-start | bytes 786436
  7.2 79.0 %all-reduce.5.cloned.1.call-start = ((), (), s32[]{:S(2)}) async-start(), calls=%async_computation | async-start | bytes 3145728 | tf_op jit(solution)/shard_map/psum | solution.py:13
  42.9 80.1 %all-reduce.7.cloned.1.call-start = ((), (), s32[]{:S(2)}) async-start(), calls=%async_computation.1 | async-start | bytes 131072 | tf_op jit(solution)/shard_map/psum | solution.py:57
  86.2 61.4 %copy-start.4 = (f32[3072,128]{1,0:T(8,128)S(1)}, f32[3072,128]{1,0:T(8,128)}, u32[]{:S(2)}) copy-start(f32[3072,128]{1,0:T(8,128)} %all-reduce.5.cloned.1.call-done) | copy-start | bytes 4718596
  90.2 175.7 %all-gather.3.cloned.1.call-start = ((), (), s32[]{:S(2)}) async-start(), calls=%async_computation.2 | async-start | bytes 7864320 | tf_op jit(solution)/shard_map/all_gather | solution.py:63
  150.3 219.5 %all-reduce.9.cloned.1.call-start = ((), (), s32[]{:S(2)}) async-start(), calls=%async_computation.3 | async-start | bytes 3145728 | tf_op jit(solution)/shard_map/psum | solution.py:13
  279.8 3.9 copy-start.3
  327.6 79.1 %all-reduce.11.cloned.1.call-start = ((), (), s32[]{:S(2)}) async-start(), calls=%async_computation.4 | async-start | bytes 131072 | tf_op jit(solution)/shard_map/psum | solution.py:57
  327.6 46.5 %copy-start.6 = (s32[3072]{0:T(1024)}, s32[3072]{0:T(1024)S(1)}, u32[]{:S(2)}) copy-start(s32[3072]{0:T(1024)S(1)} %fusion.36) | copy-start | bytes 36868
  369.9 64.3 %copy-start.5 = (f32[3072,128]{1,0:T(8,128)S(1)}, f32[3072,128]{1,0:T(8,128)}, u32[]{:S(2)}) copy-start(f32[3072,128]{1,0:T(8,128)} %all-reduce.9.cloned.1.call-done) | copy-start | bytes 4718596
  373.9 178.8 %all-gather.5.cloned.1.call-start = ((), (), s32[]{:S(2)}) async-start(), calls=%async_computation.5 | async-start | bytes 7864320 | tf_op jit(solution)/shard_map/all_gather | solution.py:63
  436.9 21.2 %copy-start.9 = (f32[1,256]{1,0:T(1,128)S(1)}, f32[1,256]{1,0:T(1,128)}, u32[]{:S(2)}) copy-start(f32[1,256]{1,0:T(1,128)} %param.15) | copy-start | bytes 3076
  436.9 37.2 %copy-start.2 = (f32[128,3072]{1,0:T(8,128)S(1)}, f32[128,3072]{1,0:T(8,128)}, u32[]{:S(2)}) copy-start(f32[128,3072]{1,0:T(8,128)} %convolution_select_fusion) | copy-start | bytes 4718596
  446.3 29.3 %copy-start.7 = (f32[1,2,256]{2,1,0:T(2,128)S(1)}, f32[1,2,256]{2,1,0:T(2,128)}, u32[]{:S(2)}) copy-start(f32[1,2,256]{2,1,0:T(2,128)} %param.20) | copy-start | bytes 6148
  446.3 29.5 %copy-start.8 = (f32[1,2,256]{2,1,0:T(2,128)S(1)}, f32[1,2,256]{2,1,0:T(2,128)}, u32[]{:S(2)}) copy-start(f32[1,2,256]{2,1,0:T(2,128)} %param.19) | copy-start | bytes 6148
  459.5 16.1 %collective-permute-start.1 = (f32[1,4]{1,0:T(1,128)S(1)}, f32[1,4]{1,0:T(1,128)S(1)}, u32[]{:S(2)}, u32[]{:S(2)}) collective-permute-start(f32[1,4]{1,0:T(1,128)S(1)} %pad_maximum_fusion.1), channel_id=1, source_target_pairs={{1,0},{2,1},{3,2},{4,3},{5,4},{6,5},{7,6},{8,7},{9,8},{10,9},{11,1... | collective-permute-start | bytes 56 | tf_op jit(solution)/shard_map/ppermute | solution.py:26
  468.2 7.6 %collective-permute-start = (f32[1,4]{1,0:T(1,128)S(1)}, f32[1,4]{1,0:T(1,128)S(1)}, u32[]{:S(2)}, u32[]{:S(2)}) collective-permute-start(f32[1,4]{1,0:T(1,128)S(1)} %pad_maximum_fusion.1), channel_id=1, source_target_pairs={{0,1},{1,2},{2,3},{3,4},{4,5},{5,6},{6,7},{7,8},{8,9},{9,10},{10,1... | collective-permute-start | bytes 56 | tf_op jit(solution)/shard_map/ppermute | solution.py:24
  476.5 6.7 %collective-permute-start.3 = (f32[1,4]{1,0:T(1,128)S(1)}, f32[1,4]{1,0:T(1,128)S(1)}, u32[]{:S(2)}, u32[]{:S(2)}) collective-permute-start(f32[1,4]{1,0:T(1,128)S(1)} %pad_maximum_fusion.2), channel_id=1, source_target_pairs={{1,0},{2,1},{3,2},{4,3},{5,4},{6,5},{7,6},{8,7},{9,8},{10,9},{11,1... | collective-permute-start | bytes 56 | tf_op jit(solution)/shard_map/ppermute | solution.py:26
  478.4 5.2 collective-permute-start.2
  607.6 43.3 %copy-start.1 = (f32[1,256,256]{2,1,0:T(8,128)S(1)}, f32[1,256,256]{2,1,0:T(8,128)}, u32[]{:S(2)}) copy-start(f32[1,256,256]{2,1,0:T(8,128)} %param.18) | copy-start | bytes 786436
Sparse Core Ops, SparseCore 0:
  43.0 43.1 all-reduce.4
  90.3 32.5 all-reduce.6
  150.4 115.4 all-gather.2
  327.7 42.1 all-reduce.8
  374.0 32.5 all-reduce.10
  437.0 115.6 all-gather.4
where the time goes:
time: 671 us; the launch traced here: 658 us
  waiting for transfers between devices  334 us (50%)
  local copies, waits for them, and re-layouts  114 us (17%)
  matrix products  101 us (15%)
  other arithmetic  57.2 us (9%)
  starting transfers between devices  21.9 us (3%)
  blocking collectives  15.4 us (2%)
  between operations  14.9 us (2%)
    all_gather x2, waiting for transfers between devices, shards(): all_factor = lax.all_gather(factor_rows, 'tm', axis=0, tiled=True)  183 us
    psum x2, waiting for transfers between devices, spread(): return lax.psum(jnp.where(mine, array, jnp.zeros_like(array)), axis)  85.5 us
    dot_general x2, matrix products, shards(): jnp.einsum('rk,tck->rtc', factor_rows, my_tiles, precision=lax.Precision....  78.5 us
    unnamed x22, local copies, waits for them, and re-layouts  76.3 us
    psum x2, waiting for transfers between devices, shards(): diag_block, rhs_segment = lax.psum((block_part, rhs_part), 'tm')  65.1 us
    another operation x6, other arithmetic, shards(): lower_block = jnp.linalg.cholesky(diag_block)  25.6 us
    another operation x4, other arithmetic, shards(): jax.scipy.linalg.solve_triangular(lower_block, panel_cols.T, lower=True)  22.4 us
    dynamic_slice x4, local copies, waits for them, and re-layouts, shards(): my_tiles = lax.dynamic_index_in_dim(grouped, factor_here, 1, keepdims=False)  18.7 us
  transfers between devices with their start and end apart: 10, of which 7 were waited for; matrix products, arithmetic and copies ran while one was open for 2% of the time, Pallas kernels for 0%

commit v1 on v0

--- a/solution.py
+++ b/solution.py
@@ -1,6 +1,10 @@
+import functools
+
 import jax
 import jax.numpy as jnp
 from jax import lax
+from jax.experimental import pallas as pl
+from jax.experimental.pallas import tpu as pltpu
 from jax.sharding import PartitionSpec as P
 
 PANELS = 2
@@ -30,18 +34,302 @@
     return cells
 
 
-def shards(
-    schur_matrix, link_rhs, hour_rhs, link_cols, link_coef, hour_inverse, couple_prev, couple_next
-):
-    rows_here = schur_matrix.shape[0]
-    tiles_here = schur_matrix.shape[1]
-    width = schur_matrix.shape[3]
+def comm_kernel(nz, ms, parts_k, own, rhs, CR, CC, D, RS, lsem, xs, xr, cs, cr, ds, dr, fs, fr, bs, br):
+    f = lax.axis_index("factor")
+    z = lax.axis_index("tm")
+    p = lax.rem(f, 2)
+    q = 1 - p
+    xx = lax.div(f, 2)
+    mate = f + 1 - 2 * p
+    over = f + 2 - 4 * xx
+    per = ms // parts_k
+    chunks = [(0, 1, 0, 2)] + [(k * per, (k + 1) * per, 2, 4) for k in range(parts_k)] + [(1, ms, 0, 2)]
+    last = len(chunks) - 1
+
+    def piece(panel, j):
+        a, b, c, d = chunks[j]
+        return CR.at[panel, a:b, c:d]
+
+    def xcopy(j):
+        return pltpu.make_async_remote_copy(
+            src_ref=piece(p, j), dst_ref=piece(p, j), send_sem=xs.at[j], recv_sem=xr.at[j],
+            device_id={"factor": over}, device_id_type=pl.DeviceIdType.MESH)
+
+    def ccopy(j, panel):
+        return pltpu.make_async_remote_copy(
+            src_ref=piece(panel, j), dst_ref=piece(panel, j), send_sem=cs.at[j], recv_sem=cr.at[j],
+            device_id={"factor": mate}, device_id_type=pl.DeviceIdType.MESH)
+
+    def zcopy(owner, d, k, step, send, recv):
+        spot = CC.at[:, pl.ds(owner * ms + k * per, per)]
+        src = CR.at[:, k * per:(k + 1) * per, f] if d == 0 else spot
+        return pltpu.make_async_remote_copy(
+            src_ref=src, dst_ref=spot, send_sem=send.at[d, k], recv_sem=recv.at[d, k],
+            device_id={"tm": z + step}, device_id_type=pl.DeviceIdType.MESH)
+
+    def fwd(d, k):
+        return zcopy(z - d, d, k, 1, fs, fr)
+
+    def bwd(d, k):
+        return zcopy(z + d, d, k, -1, bs, br)
+
+    def fwd_in(d, k):
+        return pltpu.make_async_remote_copy(
+            src_ref=CC.at[:, pl.ds((z - 1 - d) * ms + k * per, per)],
+            dst_ref=CC.at[:, pl.ds((z - 1 - d) * ms + k * per, per)],
+            send_sem=fs.at[d, k], recv_sem=fr.at[d, k],
+            device_id={"tm": z - 1}, device_id_type=pl.DeviceIdType.MESH)
+
+    def bwd_in(d, k):
+        return pltpu.make_async_remote_copy(
+            src_ref=CC.at[:, pl.ds((z + 1 + d) * ms + k * per, per)],
+            dst_ref=CC.at[:, pl.ds((z + 1 + d) * ms + k * per, per)],
+            send_sem=bs.at[d, k], recv_sem=br.at[d, k],
+            device_id={"tm": z + 1}, device_id_type=pl.DeviceIdType.MESH)
+
+    def dcopies():
+        return [
+            pltpu.make_async_remote_copy(
+                src_ref=ref, dst_ref=ref, send_sem=ds.at[i], recv_sem=dr.at[i],
+                device_id={"tm": z + 1}, device_id_type=pl.DeviceIdType.MESH)
+            for i, ref in enumerate((D, RS))]
+
+    barrier = pltpu.get_barrier_semaphore()
+    pl.semaphore_signal(barrier, inc=1, device_id={"factor": mate}, device_id_type=pl.DeviceIdType.MESH)
+    pl.semaphore_signal(barrier, inc=1, device_id={"factor": over}, device_id_type=pl.DeviceIdType.MESH)
+
+    @pl.when(z > 0)
+    def _():
+        pl.semaphore_signal(barrier, inc=1, device_id={"tm": z - 1}, device_id_type=pl.DeviceIdType.MESH)
+
+    @pl.when(z < nz - 1)
+    def _():
+        pl.semaphore_signal(barrier, inc=1, device_id={"tm": z + 1}, device_id_type=pl.DeviceIdType.MESH)
+
+    pl.semaphore_wait(barrier, 2 + jnp.where(z > 0, 1, 0) + jnp.where(z < nz - 1, 1, 0))
+
+    def own_sends(k):
+        @pl.when(z < nz - 1)
+        def _():
+            fwd(0, k).start()
+
+        @pl.when(z > 0)
+        def _():
+            bwd(0, k).start()
+
+    def diag_send():
+        @pl.when(z == 0)
+        def _():
+            one = pltpu.make_async_copy(CR.at[:, 0, 0:2], D, lsem.at[1])
+            two = pltpu.make_async_copy(rhs.at[0:8], RS, lsem.at[2])
+            one.start()
+            two.start()
+            one.wait()
+            two.wait()
+            if nz > 1:
+                for c in dcopies():
+                    c.start()
+
+    @pl.when(xx == 0)
+    def _():
+        mine = pltpu.make_async_copy(own, CR.at[p], lsem.at[0])
+        mine.start()
+        mine.wait()
+        for j in range(last + 1):
+            ccopy(j, p).start()
+            xcopy(j).start()
+        ccopy(0, q).wait_recv()
+        diag_send()
+        for j in range(1, last + 1):
+            ccopy(j, q).wait_recv()
+        for k in range(parts_k):
+            own_sends(k)
+
+    @pl.when(xx == 1)
+    def _():
+        xcopy(0).wait_recv()
+        ccopy(0, p).start()
+        ccopy(0, q).wait_recv()
+        diag_send()
+        for k in range(parts_k):
+            xcopy(k + 1).wait_recv()
+            ccopy(k + 1, p).start()
+            ccopy(k + 1, q).wait_recv()
+            own_sends(k)
+
+    local = pltpu.make_async_copy(CR.at[:, :, f], CC.at[:, pl.ds(z * ms, ms)], lsem.at[3])
+    local.start()
+
+    @pl.when(z > 0)
+    def _():
+        pair = dcopies()
+        for c in pair:
+            c.wait_recv()
+
+        @pl.when(z < nz - 1)
+        def _():
+            for c in pair:
+                c.start()
+
+    for s in range(nz - 1):
+        for k in range(parts_k):
+            @pl.when(z - 1 - s >= 0)
+            def _():
+                fwd_in(s, k).wait_recv()
+                if s + 1 < nz - 1:
+                    @pl.when(z < nz - 1)
+                    def _():
+                        fwd(s + 1, k).start()
+
+            @pl.when(z + 1 + s < nz)
+            def _():
+                bwd_in(s, k).wait_recv()
+                if s + 1 < nz - 1:
+                    @pl.when(z > 0)
+                    def _():
+                        bwd(s + 1, k).start()
+
+        if s == 0:
+            @pl.when(xx == 1)
+            def _():
+                xcopy(last).wait_recv()
+                ccopy(last, p).start()
+                ccopy(last, q).wait_recv()
+
+    for j in range(last + 1):
+        ccopy(j, p).wait_send()
+
+        @pl.when(xx == 0)
+        def _():
+            xcopy(j).wait_send()
+
+    @pl.when(z < nz - 1)
+    def _():
+        for c in dcopies():
+            c.wait_send()
+
+    for d in range(nz - 1):
+        for k in range(parts_k):
+            @pl.when((z < nz - 1) & (z - d >= 0))
+            def _():
+                fwd(d, k).wait_send()
+
+            @pl.when((z > 0) & (z + d < nz))
+            def _():
+                bwd(d, k).wait_send()
+
+    local.wait()
+
+
+def gather_columns(own, rhs, nz):
+    ms = own.shape[0]
+    w = own.shape[3]
+    parts_k = 3 if ms % 3 == 0 else 1
+    n = parts_k + 2
+    hops = max(nz - 1, 1)
+    dma = pltpu.SemaphoreType.DMA
+    anyspace = pl.BlockSpec(memory_space=pl.ANY)
+    return pl.pallas_call(
+        functools.partial(comm_kernel, nz, ms, parts_k),
+        out_shape=(
+            jax.ShapeDtypeStruct((2, ms, 4, w, w), jnp.float32),
+            jax.ShapeDtypeStruct((2, nz * ms, w, w), jnp.float32),
+            jax.ShapeDtypeStruct((2, 2, w, w), jnp.float32),
+            jax.ShapeDtypeStruct((8, w), jnp.float32),
+        ),
+        in_specs=[anyspace, anyspace],
+        out_specs=(anyspace,) * 4,
+        scratch_shapes=[
+            dma((4,)), dma((n,)), dma((n,)), dma((n,)), dma((n,)), dma((2,)), dma((2,)),
+            dma((hops, parts_k)), dma((hops, parts_k)), dma((hops, parts_k)), dma((hops, parts_k)),
+        ],
+        compiler_params=pltpu.CompilerParams(collective_id=0, has_side_effects=True),
+    )(own, rhs)
+
+
+def split(a):
+    high = a.astype(jnp.bfloat16)
+    return high, (a - high.astype(jnp.float32)).astype(jnp.bfloat16)
+
+
+def update_kernel(tiles, rows, s_ref, f_ref, g_ref, o_ref, gh_ref, gl_ref):
+    w = s_ref.shape[1]
+
+    @pl.when(pl.program_id(0) == 0)
+    def _():
+        for t in range(0, tiles, 2):
+            at = slice(t * w, (t + 2) * w)
+            gh_ref[:, at], gl_ref[:, at] = split(g_ref[:, at])
+
+    fh, fl = split(f_ref[...])
+    for t in range(0, tiles, 2):
+        gh = gh_ref[:, t * w:(t + 2) * w]
+        gl = gl_ref[:, t * w:(t + 2) * w]
+        upd = jnp.dot(fh, gh, preferred_element_type=jnp.float32)
+        upd = upd + jnp.dot(fh, gl, preferred_element_type=jnp.float32)
+        upd = upd + jnp.dot(fl, gh, preferred_element_type=jnp.float32)
+        for i in range(2):
+            at = pl.ds(t + i, rows, stride=tiles)
+            o_ref[at, :] = s_ref[at, :] - upd[:, i * w:(i + 1) * w]
+
+
+def update(flat, frow, fcol, tiles):
+    rows_here, depth = frow.shape
+    w = flat.shape[1]
+    rows = 128
+    return pl.pallas_call(
+        functools.partial(update_kernel, tiles, rows),
+        grid=(rows_here // rows,),
+        out_shape=jax.ShapeDtypeStruct(flat.shape, jnp.float32),
+        in_specs=[
+            pl.BlockSpec((rows * tiles, w), lambda i: (i, 0)),
+            pl.BlockSpec((rows, depth), lambda i: (i, 0)),
+            pl.BlockSpec(fcol.shape, lambda i: (0, 0)),
+        ],
+        out_specs=pl.BlockSpec((rows * tiles, w), lambda i: (i, 0)),
+        scratch_shapes=[pltpu.VMEM(fcol.shape, jnp.bfloat16), pltpu.VMEM(fcol.shape, jnp.bfloat16)],
+        compiler_params=pltpu.CompilerParams(vmem_limit_bytes=40 * 1024 * 1024),
+        cost_estimate=pl.CostEstimate(
+            flops=6 * rows_here * tiles * w * depth, bytes_accessed=8 * flat.size, transcendentals=0),
+    )(flat, frow, fcol)
+
+
+def eliminate(schur, rhs):
+    rows_here, tiles, _, w = schur.shape
+    nz = lax.axis_size("tm")
+    z = lax.axis_index("tm")
+    f = lax.axis_index("factor")
+    own = schur[:, 0, 0, :].reshape(rows_here // (4 * w), 4, w, w)
+    cr, cc, d, rs = gather_columns(own, rhs.reshape(-1, w), nz)
+    diag = jnp.transpose(d, (1, 2, 0, 3)).reshape(2 * w, 2 * w)
+    lower = jnp.linalg.cholesky(diag)
+    inv = jax.scipy.linalg.solve_triangular(lower, jnp.eye(2 * w, dtype=jnp.float32), lower=True)
+    inv = jnp.tril(inv)
+    hp = lax.Precision.HIGHEST
+    link = jnp.dot(inv, rs[:2].reshape(-1), precision=hp)
+    inv0, inv1 = inv[:, :w], inv[:, w:]
+    c0, c1 = cr.reshape(2, rows_here, w)
+    frow = jnp.dot(c0, inv0.T, precision=hp) + jnp.dot(c1, inv1.T, precision=hp)
+    grow = z * rows_here + jnp.arange(rows_here, dtype=jnp.int32)
+    late = jnp.arange(2 * w, dtype=jnp.int32) >= w
+    frow = jnp.where((grow < w)[:, None] & late[None, :], 0.0, frow)
+    k0, k1 = cc.reshape(2, tiles * w, w)
+    fcol = jnp.dot(inv0, k0.T, precision=hp) + jnp.dot(inv1, k1.T, precision=hp)
+    first = (jnp.arange(tiles * w, dtype=jnp.int32) < w) & (f == 0)
+    fcol = jnp.where(late[:, None] & first[None, :], 0.0, fcol)
+    trail = rhs - jnp.dot(frow, link, precision=hp)
+    out = update(schur.reshape(rows_here * tiles, w), frow, fcol, tiles)
+    return out.reshape(schur.shape), trail, link
+
+
+def panels_by_step(schur_now, rhs_now):
+    rows_here = schur_now.shape[0]
+    tiles_here = schur_now.shape[1]
+    width = schur_now.shape[3]
     factors = lax.axis_size("factor")
     row_start = lax.axis_index("tm") * rows_here
     global_rows = row_start + jnp.arange(rows_here, dtype=jnp.int32)
     factor_here = lax.axis_index("factor")
-    schur_now = schur_matrix
-    rhs_now = link_rhs
     solved = []
     for panel_id in range(PANELS):
         column_tile = panel_id // factors
@@ -68,7 +356,19 @@
         update = jnp.einsum("rk,tck->rtc", factor_rows, my_tiles, precision=lax.Precision.HIGHEST)
         schur_now = schur_now - update[:, :, None, :]
         solved.append(link_step)
-    link_values = jnp.concatenate(solved)
+    return schur_now, rhs_now, jnp.concatenate(solved)
+
+
+def shards(
+    schur_matrix, link_rhs, hour_rhs, link_cols, link_coef, hour_inverse, couple_prev, couple_next
+):
+    rows_here = schur_matrix.shape[0]
+    width = schur_matrix.shape[3]
+    factors = lax.axis_size("factor")
+    wide = factors == 4 and rows_here % (factors * width) == 0
+    wide = wide and rows_here >= 2 * factors * width and schur_matrix.shape[1] % 8 == 0
+    step = eliminate if wide else panels_by_step
+    schur_now, rhs_now, link_values = step(schur_matrix, link_rhs)
     one_hot = (
         link_cols[:, :, None] == jnp.arange(PANELS * width, dtype=jnp.int32)[None, None, :]
     ).astype(jnp.float32)

time: 671 us -> 277 us (0.41); the launches traced: 658 us -> 276 us
  waiting for transfers between devices: 334 us -> 3.63 us
  Pallas kernels: 0 us -> 166 us
  local copies, waits for them, and re-layouts: 114 us -> 15.8 us
  matrix products: 101 us -> 21.8 us
  blocking collectives: 15.4 us -> 0 us
  between operations: 14.9 us -> 2.27 us
  starting transfers between devices: 21.9 us -> 10.3 us
    all_gather x2 -> x0, waiting for transfers between devices: 183 us -> none  [shards(): all_factor = lax.all_gather(factor_rows, 'tm', axis=0, tiled=True)]
    pallas_call x0 -> x2, Pallas kernels: none -> 166 us  [the longest x1 126 us: gather_columns(): pl.pallas_call(functools.partial(comm_kernel, nz, ms, parts_k), out_shape...]
    psum x4 -> x0, waiting for transfers between devices: 151 us -> none  [the longest x2 85.5 us: spread(): return lax.psum(jnp.where(mine, array, jnp.zeros_like(array)), axis)]
    unnamed x22 -> x25, local copies, waits for them, and re-layouts: 76.3 us -> 0.75 us
    dot_general x8 -> x6, matrix products: 92.1 us -> 18.1 us  [the longest x2 9.36 us: eliminate(): frow = jnp.dot(c0, inv0.T, precision=hp) + jnp.dot(c1, inv1.T, precision=hp)]
    dynamic_slice x4 -> x0, local copies, waits for them, and re-layouts: 18.7 us -> none  [shards(): my_tiles = lax.dynamic_index_in_dim(grouped, factor_here, 1, keepdims=False)]
    reshape x2 -> x1, local copies, waits for them, and re-layouts: 16.6 us -> 0.13 us  [eliminate(): diag = jnp.transpose(d, (1, 2, 0, 3)).reshape(2 * w, 2 * w)]
    psum x2 -> x0, blocking collectives: 15.4 us -> none  [shards(): diag_block, rhs_segment = lax.psum((block_part, rhs_part), 'tm')]
  transfers between devices with their start and end apart: 10 -> 4, of which waited for: 7 -> 1; matrix products, arithmetic and copies ran while one was open for 2% -> 9% of each run, Pallas kernels for 0% -> 14%
where the time goes in v1:
time: 277 us; the launch traced here: 276 us
  Pallas kernels  166 us (60%)
  other arithmetic  55.3 us (20%)
  matrix products  21.8 us (8%)
  local copies, waits for them, and re-layouts  15.8 us (6%)
  starting transfers between devices  10.3 us (4%)
  waiting for transfers between devices  3.63 us (1%)
    pallas_call x1, Pallas kernels, gather_columns(): pl.pallas_call(functools.partial(comm_kernel, nz, ms, parts_k), out_shape...  126 us
    pallas_call x1, Pallas kernels, update(): pl.pallas_call(functools.partial(update_kernel, tiles, rows), grid=(rows_...  39.9 us
    another operation x6, other arithmetic, eliminate(): lower = jnp.linalg.cholesky(diag)  34 us
    another operation x3, other arithmetic, eliminate(): jax.scipy.linalg.solve_triangular(lower, jnp.eye(2 * w, dtype=jnp.float32...  19.7 us
    dot_general x2, matrix products, eliminate(): frow = jnp.dot(c0, inv0.T, precision=hp) + jnp.dot(c1, inv1.T, precision=hp)  9.36 us
    ppermute x2, starting transfers between devices, with_halo(): lax.ppermute(tail, axis, [(i, (i + 1) % count) for i in range(ends)])  5.97 us
    dot_general x2, matrix products, eliminate(): fcol = jnp.dot(inv0, k0.T, precision=hp) + jnp.dot(inv1, k1.T, precision=hp)  5.74 us
  transfers between devices with their start and end apart: 4, of which 1 were waited for; matrix products, arithmetic and copies ran while one was open for 9% of the time, Pallas kernels for 14%

profile of v1, /device:TPU:19, one launch (start us, length us, event | category | flops | bytes accessed | tf_op | source)
XLA Modules:
  0.0 275.6 jit_solution(17725927623323452811)
XLA Ops:
  0.7 3.4 %slice.88 = f32[3072,1,1,128]{3,2,1,0:T(1,128)} slice(f32[3072,24,1,128]{3,2,1,0:T(1,128)} %param.8), slice={[0:3072], [0:1], [0:1], [0:128]} | slice | bytes 3145728 | tf_op jit(solution)/shard_map/slice | solution.py:302
  4.1 126.5 %shard_map.103 = (f32[2,6,4,128,128]{4,3,2,1,0:T(8,128)}, f32[2,24,128,128]{3,2,1,0:T(8,128)}, f32[2,2,128,128]{3,2,1,0:T(8,128)}, f32[8,128]{1,0:T(8,128)}) custom-call(f32[6,4,128,128]{3,2,1,0:T(8,128)} %bitcast.127, f32[24,128]{1,0:T(8,128)} %bitcast.134), custom_call_target="tpu_custom_call" | custom-call | tf_op jit(solution)/shard_map/pallas_call | solution.py:232
  130.6 1.1 copy.11
  131.8 0.1 copy.12
  132.0 11.7 %cholesky.50 = f32[128,128]{1,0:T(8,128)S(1)} custom-call(f32[128,128]{1,0:T(8,128)S(1)} %cholesky.118), custom_call_target="Cholesky" | custom-call | tf_op jit(solution)/shard_map/jit(cholesky)/cholesky | solution.py:305
  143.7 9.8 %custom-call.15 = f32[1,128,128]{1,2,0:T(8,128)S(1)} custom-call(f32[1,128,128]{2,1,0:T(8,128)S(1)} %get-tuple-element.39), custom_call_target="InvertDiagBlocksLowerTriangular" | custom-call | tf_op jit(solution)/shard_map/jit(cholesky)/cholesky | solution.py:305
  153.5 0.2 constant_dynamic-update-slice_fusion.1
  153.8 0.3 convolution_subtract_fusion.1
  154.0 11.7 %cholesky.105 = f32[128,128]{1,0:T(8,128)S(1)} custom-call(f32[128,128]{1,0:T(8,128)S(1)} %convolution_subtract_fusion.1), custom_call_target="Cholesky" | custom-call | tf_op jit(solution)/shard_map/jit(cholesky)/cholesky | solution.py:305
  165.8 0.6 compare_reduce_fusion
  167.8 4.1 %while.1 = (s32[]{:T(128)}, f32[256,256]{1,0:T(8,128)S(1)}, s32[2,2]{1,0:T(2,128)S(1)}, f32[2,128,128]{2,1,0:T(8,128)S(1)}, s32[]{:T(128)}) while((s32[]{:T(128)}, f32[256,256]{1,0:T(8,128)S(1)}, s32[2,2]{1,0:T(2,128)S(1)}, f32[2,128,128]{2,1,0:T(8,128)S(1)}, s32[]{:T(128)}) %tuple.32), condition=%wide.while_cond, body=%wide.while_body.sunk | while | flops 2 | bytes 131181 | solution.py:306
  168.0 0.6 fusion.57
  168.6 1.4 bitcast_dynamic-update-slice_fusion.2
  170.0 0.6 fusion.57
  170.6 1.4 bitcast_dynamic-update-slice_fusion.2
  172.0 19.7 %custom-call.16 = f32[2,128,128]{1,2,0:T(8,128)S(1)} custom-call(f32[2,128,128]{2,1,0:T(8,128)S(1)} %get-tuple-element.18), custom_call_target="InvertDiagBlocksLowerTriangular" | custom-call | tf_op jit(solution)/shard_map/jit(_solve_triangular)/triangular_solve | solution.py:306
  191.6 0.3 fusion.11
  191.9 0.3 convolution_subtract_fusion
  192.2 0.3 fusion.20
  192.5 0.7 slice.91
  193.2 0.3 convolution_bitcast_fusion
  193.5 0.3 fusion.2
  193.8 0.3 fusion.7
  194.1 0.1 fusion.42
  194.3 1.9 collective-permute-start
  196.3 2.4 collective-permute-start.1
  198.7 0.7 maximum_select_fusion
  199.4 4.0 %fusion.39 = (f32[1,24,128,128]{3,2,1,0:T(8,128)}, f32[1,24,128,128]{3,2,1,0:T(8,128)}) fusion(f32[2,24,128,128]{3,2,1,0:T(8,128)} %get-tuple-element.9), kind=kLoop, calls=%fused_computation.75 | loop fusion | bytes 6291456 | tf_op jit(solution)/shard_map/unstack | solution.py:316
  203.5 1.4 fusion.40
  204.9 0.6 copy-done.2
  205.5 2.6 fusion.15
  208.1 4.3 %fusion.17 = f32[3072,256]{1,0:T(8,128)} fusion(f32[3072,128]{1,0:T(8,128)S(1)} %bitcast.129, f32[256,256]{1,0:T(8,128)S(1)} %copy-done.4), kind=kOutput, calls=%fused_computation.32 | convolution fusion | flops 1207959552 | bytes 4849664 | tf_op jit(solution)/shard_map/dot_general | solution.py:312
  212.4 5.1 %fusion.1.f_ref = f32[3072,256]{1,0:T(8,128)S(1)} fusion(f32[3072,256]{1,0:T(8,128)} %fusion.17, f32[3072,128]{1,0:T(8,128)} %bitcast.126, pred[256]{0:T(512)(128)(4,1)S(1)} %iota_compare_fusion.7, pred[3072]{0:T(1024)(128)(4,1)S(1)} %add_compare_fusion, f32[256,256]{1,0:T(8,128)} %maximum_select_fusion), kind=kOutput, calls=%fused_computation.5 | convolution fusion | flops 1210318848 | bytes 7998720 | tf_op jit(solution)/shard_map/dot_general | solution.py:312
  217.5 2.7 fusion.43
  220.3 0.6 sub.12
  220.9 3.1 %fusion.g_ref = f32[256,3072]{1,0:T(8,128)S(1)} fusion(f32[256,3072]{1,0:T(8,128)S(1)} %fusion.15, f32[3072,128]{1,0:T(8,128)S(1)} %bitcast.125, pred[3072]{0:T(1024)(128)(4,1)S(1)} %fusion.24, pred[256]{0:T(512)(128)(4,1)S(1)} %iota_compare_fusion.7, f32[256,256]{1,0:T(8,128)S(1)} %copy-done.5), kind=kOutput, calls=%fused_computation.3 | convolution fusion | flops 1210318848 | bytes 7998976 | tf_op jit(solution)/shard_map/dot_general | solution.py:317
  224.0 39.9 %shard_map.104 = f32[73728,128]{1,0:T(8,128)} custom-call(f32[73728,128]{1,0:T(8,128)} %bitcast.123, f32[3072,256]{1,0:T(8,128)S(1)} %fusion.1.f_ref, f32[256,3072]{1,0:T(8,128)S(1)} %fusion.g_ref), custom_call_target="tpu_custom_call" | custom-call | flops 14495514624 | bytes 75497472 | tf_op jit(solution)/shard_map/pallas_call | solution.py:280
  263.9 0.2 fusion.31
  264.1 0.1 fusion.27
  264.3 0.3 fusion.5
  264.5 0.1 fusion.41
  264.7 0.1 pad_maximum_fusion.1
  264.7 4.0 %collective-permute-start.2 = (f32[1,4]{1,0:T(1,128)S(1)}, f32[1,4]{1,0:T(1,128)S(1)}, u32[]{:S(2)}, u32[]{:S(2)}) collective-permute-start(f32[1,4]{1,0:T(1,128)S(1)} %pad_maximum_fusion.1), channel_id=1, source_target_pairs={{0,1},{1,2},{2,3},{3,4},{4,5},{5,6},{6,7},{7,8},{8,9},{9,10},{10,1... | collective-permute-start | bytes 56 | tf_op jit(solution)/shard_map/ppermute | solution.py:28
  268.8 1.9 collective-permute-start.3
  270.7 0.2 fusion.29
  270.9 3.6 %collective-permute-done.3 = f32[1,4]{1,0:T(1,128)S(1)} collective-permute-done((f32[1,4]{1,0:T(1,128)S(1)}, f32[1,4]{1,0:T(1,128)S(1)}, u32[]{:S(2)}, u32[]{:S(2)}) %collective-permute-start.3) | collective-permute-done | bytes 48 | tf_op jit(solution)/shard_map/ppermute | solution.py:30
  274.6 0.1 fusion.25
  274.7 0.9 fusion.3
  (45 shorter events, 0.6 us)
Async XLA Ops:
  0.6 193.2 %copy-start = (f32[1,256,256]{2,1,0:T(8,128)S(1)}, f32[1,256,256]{2,1,0:T(8,128)}, u32[]{:S(2)}) copy-start(f32[1,256,256]{2,1,0:T(8,128)} %param.13) | copy-start | bytes 786436
  130.6 62.9 %copy-start.9 = (f32[1,256]{1,0:T(1,128)S(1)}, f32[1,256]{1,0:T(1,128)}, u32[]{:S(2)}) copy-start(f32[1,256]{1,0:T(1,128)} %param.10) | copy-start | bytes 3076
  130.6 62.9 %copy-start.10 = (f32[1,256]{1,0:T(1,128)S(1)}, f32[1,256]{1,0:T(1,128)}, u32[]{:S(2)}) copy-start(f32[1,256]{1,0:T(1,128)} %param.12) | copy-start | bytes 3076
  130.6 62.9 %copy-start.11 = (s32[1,256]{1,0:T(1,128)S(1)}, s32[1,256]{1,0:T(1,128)}, u32[]{:S(2)}) copy-start(s32[1,256]{1,0:T(1,128)} %param.11) | copy-start | bytes 3076
  194.3 69.6 %collective-permute-start = (f32[1,4]{1,0:T(1,128)S(1)}, f32[1,4]{1,0:T(1,128)S(1)}, u32[]{:S(2)}, u32[]{:S(2)}) collective-permute-start(f32[1,4]{1,0:T(1,128)S(1)} %pad_maximum_fusion), channel_id=1, source_target_pairs={{0,1},{1,2},{2,3},{3,4},{4,5},{5,6},{6,7},{7,8},{8,9},{9,10},{10,1... | collective-permute-start | bytes 56 | tf_op jit(solution)/shard_map/ppermute | solution.py:28
  196.3 67.8 %collective-permute-start.1 = (f32[1,4]{1,0:T(1,128)S(1)}, f32[1,4]{1,0:T(1,128)S(1)}, u32[]{:S(2)}, u32[]{:S(2)}) collective-permute-start(f32[1,4]{1,0:T(1,128)S(1)} %pad_maximum_fusion), channel_id=1, source_target_pairs={{1,0},{2,1},{3,2},{4,3},{5,4},{6,5},{7,6},{8,7},{9,8},{10,9},{11,1... | collective-permute-start | bytes 56 | tf_op jit(solution)/shard_map/ppermute | solution.py:30
  199.4 4.1 %copy-start.3 = (f32[2,6,4,128,128]{4,3,2,1,0:T(8,128)S(1)}, f32[2,6,4,128,128]{4,3,2,1,0:T(8,128)}, u32[]{:S(2)}) copy-start(f32[2,6,4,128,128]{4,3,2,1,0:T(8,128)} %get-tuple-element.7) | copy-start | bytes 9437188
  203.5 2.0 copy-start.2
  203.5 2.0 copy-start.4
  217.5 2.8 %copy-start.6 = (f32[3072]{0:T(1024)S(1)}, f32[3072]{0:T(1024)}, u32[]{:S(2)}) copy-start(f32[3072]{0:T(1024)} %param.9) | copy-start | bytes 36868
  217.5 3.4 %copy-start.1 = (f32[1,24,128,128]{3,2,1,0:T(8,128)S(1)}, f32[1,24,128,128]{3,2,1,0:T(8,128)}, u32[]{:S(2)}) copy-start(f32[1,24,128,128]{3,2,1,0:T(8,128)} %get-tuple-element.32) | copy-start | bytes 4718596
  217.5 3.4 %copy-start.5 = (f32[256,256]{1,0:T(8,128)S(1)}, f32[256,256]{1,0:T(8,128)}, u32[]{:S(2)}) copy-start(f32[256,256]{1,0:T(8,128)} %maximum_select_fusion) | copy-start | bytes 786436
  224.0 39.9 %copy-start.7 = (f32[1,2,256]{2,1,0:T(2,128)S(1)}, f32[1,2,256]{2,1,0:T(2,128)}, u32[]{:S(2)}) copy-start(f32[1,2,256]{2,1,0:T(2,128)} %param.14) | copy-start | bytes 6148
  224.0 40.1 %copy-start.8 = (f32[1,2,256]{2,1,0:T(2,128)S(1)}, f32[1,2,256]{2,1,0:T(2,128)}, u32[]{:S(2)}) copy-start(f32[1,2,256]{2,1,0:T(2,128)} %param.15) | copy-start | bytes 6148
  264.7 6.0 %collective-permute-start.2 = (f32[1,4]{1,0:T(1,128)S(1)}, f32[1,4]{1,0:T(1,128)S(1)}, u32[]{:S(2)}, u32[]{:S(2)}) collective-permute-start(f32[1,4]{1,0:T(1,128)S(1)} %pad_maximum_fusion.1), channel_id=1, source_target_pairs={{0,1},{1,2},{2,3},{3,4},{4,5},{5,6},{6,7},{7,8},{8,9},{9,10},{10,1... | collective-permute-start | bytes 56 | tf_op jit(solution)/shard_map/ppermute | solution.py:28
  268.8 5.8 %collective-permute-start.3 = (f32[1,4]{1,0:T(1,128)S(1)}, f32[1,4]{1,0:T(1,128)S(1)}, u32[]{:S(2)}, u32[]{:S(2)}) collective-permute-start(f32[1,4]{1,0:T(1,128)S(1)} %pad_maximum_fusion.1), channel_id=1, source_target_pairs={{1,0},{2,1},{3,2},{4,3},{5,4},{6,5},{7,6},{8,7},{9,8},{10,9},{11,1... | collective-permute-start | bytes 56 | tf_op jit(solution)/shard_map/ppermute | solution.py:30

commit v2 on v1

--- a/solution.py
+++ b/solution.py
@@ -252,73 +252,98 @@
     return high, (a - high.astype(jnp.float32)).astype(jnp.bfloat16)
 
 
-def update_kernel(tiles, rows, s_ref, f_ref, g_ref, o_ref, gh_ref, gl_ref):
+HIGH = lax.Precision.HIGHEST
+
+
+def across(a, b):
+    return lax.dot_general(
+        a, b, (((1,), (1,)), ((), ())), precision=HIGH, preferred_element_type=jnp.float32)
+
+
+def update_kernel(tiles, rows, rows_here, s_ref, c_ref, k_ref, inv_ref, o_ref, g_ref):
     w = s_ref.shape[1]
-
-    @pl.when(pl.program_id(0) == 0)
-    def _():
+    step = pl.program_id(0)
+    inv0 = inv_ref[:, :w]
+    inv1 = inv_ref[:, w:]
+
+    @pl.when(step == 0)
+    def _():
+        owner = lax.axis_index("factor") == 0
+        out = lax.broadcasted_iota(jnp.int32, (2 * w, 2 * w), 0)
+        col = lax.broadcasted_iota(jnp.int32, (2 * w, 2 * w), 1)
         for t in range(0, tiles, 2):
             at = slice(t * w, (t + 2) * w)
-            gh_ref[:, at], gl_ref[:, at] = split(g_ref[:, at])
-
-    fh, fl = split(f_ref[...])
+            g = across(inv0, k_ref[0, at, :]) + across(inv1, k_ref[1, at, :])
+            if t == 0:
+                limit = jnp.where(owner, w, 0)
+                g = jnp.where((out >= w) & (col < limit), 0.0, g)
+            gh, gl = split(g)
+            g_ref[:2 * w, at] = gh
+            g_ref[2 * w:4 * w, at] = gl
+            g_ref[4 * w:, at] = gh
+
+    first = lax.axis_index("tm") * rows_here + step * rows
+    frow = across(c_ref[0], inv0) + across(c_ref[1], inv1)
+    row = lax.broadcasted_iota(jnp.int32, frow.shape, 0) + first
+    depth = lax.broadcasted_iota(jnp.int32, frow.shape, 1)
+    fh, fl = split(jnp.where((row < w) & (depth >= w), 0.0, frow))
+    left = jnp.concatenate([fh, fh, fl], axis=1)
     for t in range(0, tiles, 2):
-        gh = gh_ref[:, t * w:(t + 2) * w]
-        gl = gl_ref[:, t * w:(t + 2) * w]
-        upd = jnp.dot(fh, gh, preferred_element_type=jnp.float32)
-        upd = upd + jnp.dot(fh, gl, preferred_element_type=jnp.float32)
-        upd = upd + jnp.dot(fl, gh, preferred_element_type=jnp.float32)
+        upd = jnp.dot(left, g_ref[:, t * w:(t + 2) * w], preferred_element_type=jnp.float32)
         for i in range(2):
             at = pl.ds(t + i, rows, stride=tiles)
             o_ref[at, :] = s_ref[at, :] - upd[:, i * w:(i + 1) * w]
 
 
-def update(flat, frow, fcol, tiles):
-    rows_here, depth = frow.shape
+def update(flat, crow, ccol, inv, tiles):
+    rows_here = crow.shape[1]
     w = flat.shape[1]
-    rows = 128
+    rows = 2 * w
     return pl.pallas_call(
-        functools.partial(update_kernel, tiles, rows),
+        functools.partial(update_kernel, tiles, rows, rows_here),
         grid=(rows_here // rows,),
         out_shape=jax.ShapeDtypeStruct(flat.shape, jnp.float32),
         in_specs=[
             pl.BlockSpec((rows * tiles, w), lambda i: (i, 0)),
-            pl.BlockSpec((rows, depth), lambda i: (i, 0)),
-            pl.BlockSpec(fcol.shape, lambda i: (0, 0)),
+            pl.BlockSpec((2, rows, w), lambda i: (0, i, 0)),
+            pl.BlockSpec(ccol.shape, lambda i: (0, 0, 0)),
+            pl.BlockSpec(inv.shape, lambda i: (0, 0)),
         ],
         out_specs=pl.BlockSpec((rows * tiles, w), lambda i: (i, 0)),
-        scratch_shapes=[pltpu.VMEM(fcol.shape, jnp.bfloat16), pltpu.VMEM(fcol.shape, jnp.bfloat16)],
-        compiler_params=pltpu.CompilerParams(vmem_limit_bytes=40 * 1024 * 1024),
+        scratch_shapes=[pltpu.VMEM((6 * w, tiles * w), jnp.bfloat16)],
+        compiler_params=pltpu.CompilerParams(vmem_limit_bytes=48 * 1024 * 1024),
         cost_estimate=pl.CostEstimate(
-            flops=6 * rows_here * tiles * w * depth, bytes_accessed=8 * flat.size, transcendentals=0),
-    )(flat, frow, fcol)
+            flops=12 * rows_here * tiles * w * w, bytes_accessed=8 * flat.size, transcendentals=0),
+    )(flat, crow, ccol, inv)
+
+
+def lower_inverse(block):
+    eye = jnp.eye(block.shape[0], dtype=jnp.float32)
+    return jnp.tril(jax.scipy.linalg.solve_triangular(jnp.linalg.cholesky(block), eye, lower=True))
 
 
 def eliminate(schur, rhs):
     rows_here, tiles, _, w = schur.shape
     nz = lax.axis_size("tm")
     z = lax.axis_index("tm")
-    f = lax.axis_index("factor")
     own = schur[:, 0, 0, :].reshape(rows_here // (4 * w), 4, w, w)
     cr, cc, d, rs = gather_columns(own, rhs.reshape(-1, w), nz)
-    diag = jnp.transpose(d, (1, 2, 0, 3)).reshape(2 * w, 2 * w)
-    lower = jnp.linalg.cholesky(diag)
-    inv = jax.scipy.linalg.solve_triangular(lower, jnp.eye(2 * w, dtype=jnp.float32), lower=True)
-    inv = jnp.tril(inv)
-    hp = lax.Precision.HIGHEST
-    link = jnp.dot(inv, rs[:2].reshape(-1), precision=hp)
-    inv0, inv1 = inv[:, :w], inv[:, w:]
-    c0, c1 = cr.reshape(2, rows_here, w)
-    frow = jnp.dot(c0, inv0.T, precision=hp) + jnp.dot(c1, inv1.T, precision=hp)
+    top = lower_inverse(d[0, 0])
+    side = jnp.dot(d[0, 1], top.T, precision=HIGH)
+    low = lower_inverse(d[1, 1] - jnp.dot(side, side.T, precision=HIGH))
+    mixed = -jnp.dot(low, jnp.dot(side, top, precision=HIGH), precision=HIGH)
+    zero = jnp.zeros((w, w), jnp.float32)
+    inv = jnp.concatenate(
+        [jnp.concatenate([top, zero], axis=1), jnp.concatenate([mixed, low], axis=1)], axis=0)
+    link = jnp.dot(inv, rs[:2].reshape(-1), precision=HIGH)
+    crow = cr.reshape(2, rows_here, w)
+    out = update(schur.reshape(rows_here * tiles, w), crow, cc.reshape(2, tiles * w, w), inv, tiles)
+    back = jnp.dot(link, inv, precision=HIGH)
+    early = jnp.dot(link[:w], top, precision=HIGH)
+    both = jnp.dot(jnp.stack([back[:w], early]), crow[0].T, precision=HIGH)
+    rest = jnp.dot(crow[1], back[w:], precision=HIGH)
     grow = z * rows_here + jnp.arange(rows_here, dtype=jnp.int32)
-    late = jnp.arange(2 * w, dtype=jnp.int32) >= w
-    frow = jnp.where((grow < w)[:, None] & late[None, :], 0.0, frow)
-    k0, k1 = cc.reshape(2, tiles * w, w)
-    fcol = jnp.dot(inv0, k0.T, precision=hp) + jnp.dot(inv1, k1.T, precision=hp)
-    first = (jnp.arange(tiles * w, dtype=jnp.int32) < w) & (f == 0)
-    fcol = jnp.where(late[:, None] & first[None, :], 0.0, fcol)
-    trail = rhs - jnp.dot(frow, link, precision=hp)
-    out = update(schur.reshape(rows_here * tiles, w), frow, fcol, tiles)
+    trail = rhs - jnp.where(grow < w, both[1], both[0] + rest)
     return out.reshape(schur.shape), trail, link
 
 

time: 277 us -> 260 us (0.939)
  matrix products: 21.8 us -> 10.6 us
  local copies, waits for them, and re-layouts: 15.8 us -> 7.57 us
  Pallas kernels: 166 us -> 174 us
  other arithmetic: 55.3 us -> 51.2 us
  waiting for transfers between devices: 3.63 us -> 0.57 us
    dot_general x6 -> x9, matrix products: 18.1 us -> 7.67 us  [the longest x2 1.87 us: eliminate(): mixed = -jnp.dot(low, jnp.dot(side, top, precision=HIGH), precision=HIGH)]
    another operation x11 -> x1, local copies, waits for them, and re-layouts: 9.46 us -> 0.01 us  [eliminate(): both = jnp.dot(jnp.stack([back[:w], early]), crow[0].T, precision=HIGH)]
    pallas_call x1, Pallas kernels: 39.9 us -> 48 us  [update(): pl.pallas_call(functools.partial(update_kernel, tiles, rows, rows_here),...]
    another operation x9 -> x10, other arithmetic: 53.7 us -> 48.2 us  [the longest x6 25.6 us: lower_inverse(): jnp.linalg.cholesky(block)]
    ppermute x2, waiting for transfers between devices: 3.63 us -> 0.01 us  [with_halo(): lax.ppermute(head, axis, [((i + 1) % count, i) for i in range(ends)])]
    ppermute x2, starting transfers between devices: 5.97 us -> 9.08 us  [with_halo(): lax.ppermute(tail, axis, [(i, (i + 1) % count) for i in range(ends)])]
  transfers between devices with their start and end apart: 4 -> 4, of which waited for: 1 -> 1; matrix products, arithmetic and copies ran while one was open for 9% -> 2% of each run, Pallas kernels for 14% -> 19%
where the time goes in v2:
time: 260 us; the launch traced here: 258 us
  Pallas kernels  174 us (67%)
  other arithmetic  51.2 us (20%)
  starting transfers between devices  12.9 us (5%)
  matrix products  10.6 us (4%)
  local copies, waits for them, and re-layouts  7.57 us (3%)
    pallas_call x1, Pallas kernels, gather_columns(): pl.pallas_call(functools.partial(comm_kernel, nz, ms, parts_k), out_shape...  126 us
    pallas_call x1, Pallas kernels, update(): pl.pallas_call(functools.partial(update_kernel, tiles, rows, rows_here),...  48 us
    another operation x6, other arithmetic, lower_inverse(): jnp.linalg.cholesky(block)  25.6 us
    another operation x4, other arithmetic, lower_inverse(): jax.scipy.linalg.solve_triangular(jnp.linalg.cholesky(block), eye, lower=...  22.5 us
    ppermute x2, starting transfers between devices, with_halo(): lax.ppermute(tail, axis, [(i, (i + 1) % count) for i in range(ends)])  9.08 us
  transfers between devices with their start and end apart: 4, of which 1 were waited for; matrix products, arithmetic and copies ran while one was open for 2% of the time, Pallas kernels for 19%

profile of v2, /device:TPU:19, one launch (start us, length us, event | category | flops | bytes accessed | tf_op | source)
XLA Modules:
  0.0 258.2 jit_solution(11883724481003230397)
XLA Ops:
  0.6 3.4 %slice.70 = f32[3072,1,1,128]{3,2,1,0:T(1,128)} slice(f32[3072,24,1,128]{3,2,1,0:T(1,128)} %param.11), slice={[0:3072], [0:1], [0:1], [0:128]} | slice | bytes 3145728 | tf_op jit(solution)/shard_map/slice | solution.py:329
  4.1 126.5 %shard_map.103 = (f32[2,6,4,128,128]{4,3,2,1,0:T(8,128)}, f32[2,24,128,128]{3,2,1,0:T(8,128)}, f32[2,2,128,128]{3,2,1,0:T(8,128)}, f32[8,128]{1,0:T(8,128)}) custom-call(f32[6,4,128,128]{3,2,1,0:T(8,128)} %bitcast.131, f32[24,128]{1,0:T(8,128)} %bitcast.135), custom_call_target="tpu_custom_call" | custom-call | tf_op jit(solution)/shard_map/pallas_call | solution.py:232
  130.6 1.1 copy.11
  131.7 0.1 copy.12
  131.8 11.7 %cholesky.44 = f32[128,128]{1,0:T(8,128)S(1)} custom-call(f32[128,128]{1,0:T(8,128)S(1)} %fusion.12), custom_call_target="Cholesky" | custom-call | tf_op jit(solution)/shard_map/jit(cholesky)/cholesky | solution.py:322
  143.5 0.6 compare_reduce_fusion.1
  144.2 0.7 fusion.10
  144.9 9.8 %custom-call.6 = f32[1,128,128]{1,2,0:T(8,128)S(1)} custom-call(f32[1,128,128]{2,1,0:T(8,128)S(1)} %fusion.10), custom_call_target="InvertDiagBlocksLowerTriangular" | custom-call | tf_op jit(solution)/shard_map/jit(_solve_triangular)/triangular_solve | solution.py:322
  154.7 0.3 convolution_select_fusion.1
  155.0 1.1 fusion.15
  156.1 1.3 convolution_subtract_fusion
  157.3 0.8 fusion.51
  158.2 0.7 slice.74
  158.8 0.7 copy.15
  159.6 1.5 fusion.14
  161.1 12.5 %cholesky.55 = f32[128,128]{1,0:T(8,128)S(1)} custom-call(f32[128,128]{1,0:T(8,128)} %fusion.14), custom_call_target="Cholesky" | custom-call | tf_op jit(solution)/shard_map/jit(cholesky)/cholesky | solution.py:322
  173.6 0.6 compare_reduce_fusion
  174.3 1.3 fusion.11
  175.6 10.8 %custom-call.7 = f32[1,128,128]{1,2,0:T(8,128)S(1)} custom-call(f32[1,128,128]{2,1,0:T(8,128)} %fusion.11), custom_call_target="InvertDiagBlocksLowerTriangular" | custom-call | tf_op jit(solution)/shard_map/jit(_solve_triangular)/triangular_solve | solution.py:322
  186.4 0.3 convolution_select_fusion
  186.7 1.0 convolution_negate_fusion
  187.7 0.3 fusion.46
  188.1 0.3 fusion
  188.3 0.3 fusion.5
  188.7 0.1 fusion.50
  188.8 0.1 pad_maximum_fusion
  188.9 1.9 collective-permute-start.1
  190.8 4.5 %collective-permute-start = (f32[1,4]{1,0:T(1,128)S(1)}, f32[1,4]{1,0:T(1,128)S(1)}, u32[]{:S(2)}, u32[]{:S(2)}) collective-permute-start(f32[1,4]{1,0:T(1,128)S(1)} %pad_maximum_fusion), channel_id=1, source_target_pairs={{0,1},{1,2},{2,3},{3,4},{4,5},{5,6},{6,7},{7,8},{8,9},{9,10},{10,1... | collective-permute-start | bytes 56 | tf_op jit(solution)/shard_map/ppermute | solution.py:28
  195.3 0.2 fusion.35
  195.5 0.8 select_maximum_fusion.inv_ref
  196.3 0.2 fusion.41
  196.4 0.2 fusion.47
  196.7 1.4 fusion.39
  198.1 1.4 fusion.27
  199.6 0.6 select_subtract_fusion
  200.2 0.9 copy-done.2
  201.1 48.0 %shard_map.104 = f32[73728,128]{1,0:T(8,128)} custom-call(f32[73728,128]{1,0:T(8,128)} %bitcast.129, f32[2,3072,128]{2,1,0:T(8,128)S(1)} %bitcast.128, f32[2,3072,128]{2,1,0:T(8,128)} %bitcast.134, f32[256,256]{1,0:T(8,128)S(1)} %copy-done.2), custom_call_target="tpu_custom_call" | custom-call | flops 14495514624 | bytes 75497472 | tf_op jit(solution)/shard_map/pallas_call | solution.py:302
  249.1 0.1 fusion.21
  249.3 0.2 fusion.25
  249.5 0.3 fusion.3
  249.7 0.1 fusion.49
  249.9 0.1 pad_maximum_fusion.1
  249.9 1.9 collective-permute-start.3
  251.9 4.5 %collective-permute-start.2 = (f32[1,4]{1,0:T(1,128)S(1)}, f32[1,4]{1,0:T(1,128)S(1)}, u32[]{:S(2)}, u32[]{:S(2)}) collective-permute-start(f32[1,4]{1,0:T(1,128)S(1)} %pad_maximum_fusion.1), channel_id=1, source_target_pairs={{0,1},{1,2},{2,3},{3,4},{4,5},{5,6},{6,7},{7,8},{8,9},{9,10},{10,1... | collective-permute-start | bytes 56 | tf_op jit(solution)/shard_map/ppermute | solution.py:28
  256.4 0.1 fusion.19
  256.6 0.6 collective-permute-done.2
  257.1 0.2 fusion.23
  257.3 0.9 fusion.1
  (30 shorter events, 0.3 us)
Async XLA Ops:
  0.6 187.7 %copy-start = (f32[1,256,256]{2,1,0:T(8,128)S(1)}, f32[1,256,256]{2,1,0:T(8,128)}, u32[]{:S(2)}) copy-start(f32[1,256,256]{2,1,0:T(8,128)} %param.16) | copy-start | bytes 786436
  130.5 57.5 %copy-start.7 = (f32[1,256]{1,0:T(1,128)S(1)}, f32[1,256]{1,0:T(1,128)}, u32[]{:S(2)}) copy-start(f32[1,256]{1,0:T(1,128)} %param.13) | copy-start | bytes 3076
  130.5 57.5 %copy-start.8 = (f32[1,256]{1,0:T(1,128)S(1)}, f32[1,256]{1,0:T(1,128)}, u32[]{:S(2)}) copy-start(f32[1,256]{1,0:T(1,128)} %param.15) | copy-start | bytes 3076
  130.5 57.5 %copy-start.9 = (s32[1,256]{1,0:T(1,128)S(1)}, s32[1,256]{1,0:T(1,128)}, u32[]{:S(2)}) copy-start(s32[1,256]{1,0:T(1,128)} %param.14) | copy-start | bytes 3076
  131.7 23.3 %copy-start.3 = (f32[2,2,128,128]{2,3,1,0:T(8,128)}, f32[2,2,128,128]{2,3,1,0:T(8,128)S(1)}, u32[]{:S(2)}) copy-start(f32[2,2,128,128]{2,3,1,0:T(8,128)S(1)} %copy.11) | copy-start | bytes 786436
  156.1 40.4 %copy-start.1 = (f32[2,6,4,128,128]{4,3,2,1,0:T(8,128)S(1)}, f32[2,6,4,128,128]{4,3,2,1,0:T(8,128)}, u32[]{:S(2)}) copy-start(f32[2,6,4,128,128]{4,3,2,1,0:T(8,128)} %get-tuple-element.9) | copy-start | bytes 9437188
  188.9 60.3 %collective-permute-start.1 = (f32[1,4]{1,0:T(1,128)S(1)}, f32[1,4]{1,0:T(1,128)S(1)}, u32[]{:S(2)}, u32[]{:S(2)}) collective-permute-start(f32[1,4]{1,0:T(1,128)S(1)} %pad_maximum_fusion), channel_id=1, source_target_pairs={{1,0},{2,1},{3,2},{4,3},{5,4},{6,5},{7,6},{8,7},{9,8},{10,9},{11,1... | collective-permute-start | bytes 56 | tf_op jit(solution)/shard_map/ppermute | solution.py:30
  190.8 58.5 %collective-permute-start = (f32[1,4]{1,0:T(1,128)S(1)}, f32[1,4]{1,0:T(1,128)S(1)}, u32[]{:S(2)}, u32[]{:S(2)}) collective-permute-start(f32[1,4]{1,0:T(1,128)S(1)} %pad_maximum_fusion), channel_id=1, source_target_pairs={{0,1},{1,2},{2,3},{3,4},{4,5},{5,6},{6,7},{7,8},{8,9},{9,10},{10,1... | collective-permute-start | bytes 56 | tf_op jit(solution)/shard_map/ppermute | solution.py:28
  196.7 2.9 %copy-start.4 = (f32[3072]{0:T(1024)S(1)}, f32[3072]{0:T(1024)}, u32[]{:S(2)}) copy-start(f32[3072]{0:T(1024)} %param.12) | copy-start | bytes 36868
  200.2 0.9 copy-start.2
  201.1 48.0 %copy-start.5 = (f32[1,2,256]{2,1,0:T(2,128)S(1)}, f32[1,2,256]{2,1,0:T(2,128)}, u32[]{:S(2)}) copy-start(f32[1,2,256]{2,1,0:T(2,128)} %param.18) | copy-start | bytes 6148
  201.1 48.1 %copy-start.6 = (f32[1,2,256]{2,1,0:T(2,128)S(1)}, f32[1,2,256]{2,1,0:T(2,128)}, u32[]{:S(2)}) copy-start(f32[1,2,256]{2,1,0:T(2,128)} %param.17) | copy-start | bytes 6148
  249.9 6.5 %collective-permute-start.3 = (f32[1,4]{1,0:T(1,128)S(1)}, f32[1,4]{1,0:T(1,128)S(1)}, u32[]{:S(2)}, u32[]{:S(2)}) collective-permute-start(f32[1,4]{1,0:T(1,128)S(1)} %pad_maximum_fusion.1), channel_id=1, source_target_pairs={{1,0},{2,1},{3,2},{4,3},{5,4},{6,5},{7,6},{8,7},{9,8},{10,9},{11,1... | collective-permute-start | bytes 56 | tf_op jit(solution)/shard_map/ppermute | solution.py:30
  251.9 5.2 %collective-permute-start.2 = (f32[1,4]{1,0:T(1,128)S(1)}, f32[1,4]{1,0:T(1,128)S(1)}, u32[]{:S(2)}, u32[]{:S(2)}) collective-permute-start(f32[1,4]{1,0:T(1,128)S(1)} %pad_maximum_fusion.1), channel_id=1, source_target_pairs={{0,1},{1,2},{2,3},{3,4},{4,5},{5,6},{6,7},{7,8},{8,9},{9,10},{10,1... | collective-permute-start | bytes 56 | tf_op jit(solution)/shard_map/ppermute | solution.py:28
